TPU v7x, 768 devices: a whole 4x8x12 slice. The times are simulated.
768 devices in a mesh: section: 48 (over y, z_hi, core), mp: 16 (over z_lo, x).
Axes of the slice: x: 4, y: 8, z: 12 (z_hi: 3, z_lo: 4; z = z_hi * 4 + z_lo), core: 2. Of those that a mesh axis runs over, the one named last changes fastest.
Arguments:
- queries: bfloat16 [48, 256, 4096], P('section', None, 'mp'), may hold values from -80 to 80
- encoded: bfloat16 [48, 256, 4096], P('section', None, 'mp'), may hold values from -5 to 5
- key_weight: bfloat16 [48, 4096, 4096], P('section', None, 'mp'), may hold values from -1 to 2
- value_weight: bfloat16 [48, 4096, 4096], P('section', None, 'mp'), may hold values from -0.09375 to 0.09375
- owner: int32 [8], replicated, may hold values from 0 to 47, as said below
Outputs:
- passed: bfloat16 [48, 256, 4096], P('section', None, 'mp')
Inputs may be any that keep to these rules, and one draw needn't show every extreme that they name: The 8 entries are distinct sections; owner[m] is the section whose block of encoded serves micro-batch m. Section 47 is always among them, and micro-batch 0 is always served by section 0.
All inputs are finite; a program needn't handle non-finite values.
Results may differ from a plain program's by a relative error of at most 0.011.
Values may be sent and summed in bfloat16 or wider, within the bound.
A program may use at most 32 MiB of HBM per device.

v0:
```python
import jax
import jax.numpy as jnp
from jax import lax
from jax.sharding import PartitionSpec as P

HEAD_DIM = 256
MICRO = 8


def from_behind(block, axis, distance):
    devices = range(lax.axis_size(axis))
    route = [((i - distance) % len(devices), i) for i in devices]
    return lax.ppermute(block, axis, route)


def per_device(queries, encoded, key_weight, value_weight, owner):
    here = lax.axis_index("section")
    mine = here % MICRO
    micro_ids = jnp.arange(MICRO, dtype=jnp.int32)
    target = jnp.sum(jnp.where(micro_ids == mine, owner, 0))
    piece = lax.all_gather(encoded, "section", axis=0, tiled=True)
    positions = jnp.arange(piece.shape[0], dtype=jnp.int32)
    keep = (positions == target)[:, None, None]
    chosen = jnp.sum(jnp.where(keep, piece, jnp.zeros_like(piece)), axis=0)
    w_key = key_weight[0]
    w_value = value_weight[0]
    width = w_key.shape[1]
    enc_rows = chosen.shape[0]
    piece = lax.all_gather(chosen, "mp", axis=1, tiled=True)
    keys = jnp.dot(piece, w_key, preferred_element_type=jnp.float32)
    values = jnp.dot(piece, w_value, preferred_element_type=jnp.float32)
    keys = keys.astype(jnp.bfloat16)
    values = values.astype(jnp.bfloat16)
    local_heads = width // HEAD_DIM
    dec_rows = queries.shape[1]
    q_heads = queries[0].reshape(dec_rows, local_heads, HEAD_DIM)
    k_heads = keys.reshape(enc_rows, local_heads, HEAD_DIM)
    v_heads = values.reshape(enc_rows, local_heads, HEAD_DIM)
    scores = jnp.einsum(
        "thd,shd->hts", q_heads, k_heads, preferred_element_type=jnp.float32
    ) * HEAD_DIM ** (-0.5)
    probs = jax.nn.softmax(scores, axis=-1).astype(jnp.bfloat16)
    context = jnp.einsum("hts,shd->thd", probs, v_heads, preferred_element_type=jnp.float32)
    context = context.reshape(1, dec_rows, width).astype(jnp.bfloat16)
    return from_behind(context, "section", 1)


def solution(mesh):
    placed = (
        P("section", None, "mp"),
        P("section", None, "mp"),
        P("section", None, "mp"),
        P("section", None, "mp"),
        P(),
    )
    return jax.shard_map(
        per_device, mesh=mesh, in_specs=placed, out_specs=P("section", None, "mp"), check_vma=False
    )
```

profile of v0, /device:TPU:102, one launch (start us, length us, event | category | flops | bytes accessed | tf_op | source)
XLA Modules:
  0.0 261.4 jit_solution(9271522223679264059)
XLA Ops:
  6.5 0.0 copy-start
  6.5 0.0 all-gather.3.cloned.1.call-start
  6.5 0.7 all-gather.3.cloned.1.call-update
  7.3 0.0 all-gather.5.cloned.1.call-start
  7.3 1.3 fusion.19
  8.6 0.6 iota_compare_fusion
  9.3 0.0 copy-start.1
  9.3 127.8 %all-gather.3.cloned.1.call-done = bf16[48,256,256]{2,1,0:T(8,128)(2,1)} async-done(((bf16[1,256,256]{2,1,0:T(8,128)(2,1)}), bf16[48,256,256]{2,1,0:T(8,128)(2,1)}) %all-gather.3.cloned.1.call-update) | async-done | bytes 6291472 | tf_op jit(solution)/shard_map/all_gather | solution.py:21
  137.1 4.5 %select_reduce_fusion = bf16[256,256]{1,0:T(8,128)(2,1)} fusion(bf16[48,256,256]{2,1,0:T(8,128)(2,1)} %all-gather.3.cloned.1.call-done, pred[48]{0:T(512)(128)(4,1)S(1)} %iota_compare_fusion), kind=kLoop, calls=%fused_computation | loop fusion | flops 6225920 | bytes 6422576 | tf_op jit(solution)/shard_map/reduce_sum | solution.py:24
  141.6 0.0 all-gather.5.cloned.1.call-update
  141.6 91.8 %all-gather.5.cloned.1.call-done = bf16[256,4096]{1,0:T(8,128)(2,1)} async-done(((bf16[256,256]{1,0:T(8,128)(2,1)}), bf16[256,4096]{1,0:T(8,128)(2,1)}) %all-gather.5.cloned.1.call-update) | async-done | bytes 2097168 | tf_op jit(solution)/shard_map/all_gather | solution.py:29
  233.4 0.0 copy-done
  233.5 0.0 copy-done.1
  233.5 2.5 fusion.20
  236.0 0.1 fusion.15
  236.0 3.2 %fusion.10 = bf16[1,256,256]{1,2,0:T(8,128)(2,1)S(1)} fusion(bf16[256,4096]{1,0:T(8,128)(2,1)} %all-gather.5.cloned.1.call-done, bf16[1,4096,256]{2,1,0:T(8,128)(2,1)} %param.8, f32[256,256]{1,0:T(8,128)S(1)} %get-tuple-element.6, f32[256]{0:T(256)S(1)} %fusion.15, f32[256]{0:T(256)S(1)} %get-tuple-element.5), kind=kOutput, calls=%fused_computation.9 | convolution fusion | flops 570753024 | bytes 4589568 | tf_op jit(solution)/shard_map/hts,shd->thd/dot_general | solution.py:43
  239.2 1.9 collective-permute-start
  241.2 12.7 %collective-permute-done = bf16[1,256,256]{1,2,0:T(8,128)(2,1)S(1)} collective-permute-done((bf16[1,256,256]{1,2,0:T(8,128)(2,1)S(1)}, bf16[1,256,256]{1,2,0:T(8,128)(2,1)S(1)}, u32[]{:S(2)}, u32[]{:S(2)}) %collective-permute-start) | collective-permute-done | bytes 131104 | tf_op jit(solution)/shard_map/ppermute | solution.py:13
  253.8 0.8 copy.7
Async XLA Ops:
  6.5 226.9 %copy-start = (bf16[1,4096,256]{2,1,0:T(8,128)(2,1)S(1)}, bf16[1,4096,256]{2,1,0:T(8,128)(2,1)}, u32[]{:S(2)}) copy-start(bf16[1,4096,256]{2,1,0:T(8,128)(2,1)} %param.7) | copy-start | bytes 6291460
  6.5 130.5 %all-gather.3.cloned.1.call-start = ((), (), s32[]{:S(2)}) async-start(), calls=%async_computation | async-start | bytes 6422528 | tf_op jit(solution)/shard_map/all_gather | solution.py:21
  7.3 226.2 %all-gather.5.cloned.1.call-start = ((), (), s32[]{:S(2)}) async-start(), calls=%async_computation.1 | async-start | bytes 2228224 | tf_op jit(solution)/shard_map/all_gather | solution.py:29
  9.3 224.2 %copy-start.1 = (bf16[1,256,256]{2,1,0:T(8,128)(2,1)S(1)}, bf16[1,256,256]{2,1,0:T(8,128)(2,1)}, u32[]{:S(2)}) copy-start(bf16[1,256,256]{2,1,0:T(8,128)(2,1)} %param.5) | copy-start | bytes 393220
  239.2 14.6 %collective-permute-start = (bf16[1,256,256]{1,2,0:T(8,128)(2,1)S(1)}, bf16[1,256,256]{1,2,0:T(8,128)(2,1)S(1)}, u32[]{:S(2)}, u32[]{:S(2)}) collective-permute-start(bf16[1,256,256]{1,2,0:T(8,128)(2,1)S(1)} %fusion.10), channel_id=1, source_target_pairs={{752,0},{0,16},{16,32},{32,48},{48,64},{64,80},{80,96},{96,112},{1... | collective-permute-start | bytes 393224 | tf_op jit(solution)/shard_map/ppermute | solution.py:13
Sparse Core Ops, SparseCore 0:
  11.4 125.6 all-gather.2
  141.7 91.6 all-gather.4
where the time goes:
time: 262 us; the launch traced here: 261 us
  waiting for transfers between devices  233 us (89%)
  between operations  13.5 us (5%)
  other arithmetic  6.54 us (2%)
  matrix products  5.69 us (2%)
    all_gather x1, waiting for transfers between devices, per_device(): piece = lax.all_gather(encoded, 'section', axis=0, tiled=True)  128 us
    all_gather x1, waiting for transfers between devices, per_device(): piece = lax.all_gather(chosen, 'mp', axis=1, tiled=True)  91.8 us
    ppermute x1, waiting for transfers between devices, from_behind(): return lax.ppermute(block, axis, route)  12.7 us
  transfers between devices with their start and end apart: 3, of which 3 were waited for; matrix products, arithmetic and copies ran while one was open for 1% of the time, Pallas kernels for 0%

commit v1 on v0

v1 whole, which is shorter than its diff:
```python
import jax
import jax.numpy as jnp
from jax import lax
from jax.experimental import pallas as pl
from jax.experimental.pallas import tpu as pltpu
from jax.sharding import PartitionSpec as P

MESH = pl.DeviceIdType.MESH
HEAD_DIM = 256
MICRO = 8
NY, NZH, NC = 8, 3, 2
NZL, NX = 4, 4
PLANE = NY * NC
ROWS = 256
PIECE = ROWS // PLANE
HALF = 128
CHUNKS = 4
F32 = jnp.float32
BF16 = jnp.bfloat16


def kernel(q_hbm, e_hbm, wk_hbm, wv_hbm, owner_hbm, out_hbm,
           owner, q, wk, wv, p0, p1, c0, c1, f, e, acck, accv, ctx,
           own_sem, q_sem, w_sem, s1_send, s1_recv, s2_send, s2_recv, s3_send, s3_recv,
           z_send, x_send, g_recv, o_send, o_recv):
    sec = lax.axis_index("section")
    mp = lax.axis_index("mp")
    y, zh, c = lax.div(sec, 6), lax.rem(lax.div(sec, 2), 3), lax.rem(sec, 2)
    zl, x = lax.div(mp, 4), lax.rem(mp, 4)
    place = y * 2 + c
    right = zl * 4 + lax.rem(x + 1, 4)
    left = zl * 4 + lax.rem(x + 3, 4)
    nxt = lax.rem(sec + 1, 48)
    prv = lax.rem(sec + 47, 48)
    p, cc = (p0, p1), (c0, c1)

    def plane_section(t):
        return lax.div(t, 2) * 6 + zh * 2 + lax.rem(t, 2)

    def beside(k):
        return y * 6 + lax.rem(zh + k, 3) * 2 + c

    def line(k):
        if k == 0:
            return zl
        if k == 1:
            return zl + 1 - 2 * lax.rem(zl, 2)
        if k == 2:
            return zl + 2 - 4 * lax.div(zl, 2)
        return 3 - zl

    def remote(src, dst, ssem, rsem, section, model):
        return pltpu.make_async_remote_copy(
            src_ref=src, dst_ref=dst, send_sem=ssem, recv_sem=rsem,
            device_id=(section, model), device_id_type=MESH)

    own_copy = pltpu.make_async_copy(owner_hbm, owner, own_sem)
    own_copy.start()
    for h in range(2):
        pltpu.make_async_copy(
            e_hbm.at[0, pl.ds(place * PIECE, PIECE), pl.ds(h * HALF, HALF)],
            p[h].at[place], s1_recv.at[h]).start()
    loads = [pltpu.make_async_copy(q_hbm.at[0], q, q_sem)]
    for h in range(2):
        loads.append(pltpu.make_async_copy(wk_hbm.at[:, h], wk.at[h], w_sem.at[0, h]))
        loads.append(pltpu.make_async_copy(wv_hbm.at[:, h], wv.at[h], w_sem.at[1, h]))

    barrier = pltpu.get_barrier_semaphore()

    def greet(section, model):
        pl.semaphore_signal(barrier, inc=1, device_id=(section, model), device_id_type=MESH)

    @pl.loop(1, PLANE)
    def _(i):
        greet(plane_section(lax.rem(place + i, PLANE)), mp)

    greet(beside(1), mp)
    greet(beside(2), mp)
    for k in (1, 2, 3):
        greet(sec, line(k) * 4 + x)
    greet(sec, right)
    greet(sec, left)
    greet(prv, mp)
    for load in loads:
        load.start()
    acck[...] = jnp.zeros_like(acck)
    accv[...] = jnp.zeros_like(accv)
    pl.semaphore_wait(barrier, PLANE - 1 + 2 + 3 + 2 + 1)

    for h in range(2):
        @pl.loop(1, PLANE)
        def _(i):
            t = lax.rem(place + i, PLANE)
            remote(e_hbm.at[0, pl.ds(t * PIECE, PIECE), pl.ds(h * HALF, HALF)],
                   p[h].at[place], s1_send.at[h], s1_recv.at[h], plane_section(t), mp).start()

    own_copy.wait()
    at_place, at_zh = [], []
    for m in range(MICRO):
        o = owner[m]
        at_place.append(lax.div(o, 6) * 2 + lax.rem(o, 2))
        at_zh.append(lax.rem(lax.div(o, 2), 3))
    for h in range(2):
        pltpu.make_async_copy(p[h], p[h], s1_recv.at[h]).wait()
        for m in range(MICRO):
            cc[h][zh, m] = p[h][at_place[m]]
        for k in (1, 2):
            remote(cc[h].at[zh], cc[h].at[zh], s2_send.at[h], s2_recv.at[h], beside(k), mp).start()

    for h in range(2):
        pltpu.make_async_copy(cc[h].at[pl.ds(0, 2)], cc[h].at[pl.ds(0, 2)], s2_recv.at[h]).wait()
        for m in range(MICRO):
            f[h, m] = cc[h][at_zh[m], m]
        rows = pl.ds(place * PIECE, PIECE)

        @pl.loop(1, PLANE)
        def _(i):
            t = lax.rem(place + i, PLANE)
            s = plane_section(t)
            remote(f.at[h, lax.rem(s, MICRO)], e.at[h, mp, rows], s3_send.at[h], s3_recv.at[h], s, mp).start()

        e[h, mp, rows] = f[h, lax.rem(sec, MICRO)]

    def block(h, j):
        return e.at[h, j]

    def ready(h):
        pltpu.make_async_copy(e.at[h, mp, pl.ds(0, ROWS - PIECE)],
                              e.at[h, mp, pl.ds(0, ROWS - PIECE)], s3_recv.at[h]).wait()
        for k in (1, 2, 3):
            remote(block(h, mp), block(h, mp), z_send.at[h], g_recv.at[h, mp], sec, line(k) * 4 + x).start()

    def arrived(h, j):
        pltpu.make_async_copy(block(h, j), block(h, j), g_recv.at[h, j]).wait()

    def to_x(h, j, model):
        remote(block(h, j), block(h, j), x_send.at[h], g_recv.at[h, j], sec, model).start()

    def stage_a(h, k):
        j = line(k) * 4 + x
        if k > 0:
            arrived(h, j)
        to_x(h, j, right)
        to_x(h, j, left)

    def stage_b(h, k):
        j = line(k) * 4
        from_left = j + lax.rem(x + 3, 4)
        from_right = j + lax.rem(x + 1, 4)
        if k % 2 == 0:
            arrived(h, from_left)
            to_x(h, from_left, right)
            arrived(h, from_right)
        else:
            arrived(h, from_right)
            to_x(h, from_right, left)
            arrived(h, from_left)

    def stage_c(h, k):
        j = line(k) * 4
        arrived(h, j + lax.rem(x + 2, 4))
        left_side = jnp.concatenate([e[h, j + i] for i in range(NX)], axis=1)
        for w, acc in ((wk, acck), (wv, accv)):
            rows = w[h, pl.ds(j, NX)].reshape(NX * HALF, HEAD_DIM)
            acc[...] += jnp.dot(left_side, rows, preferred_element_type=F32)

    for h in range(2):
        ready(h)
        if h == 0:
            stage_a(0, 0)
            for load in loads:
                load.wait()
    steps = [(h, k) for h in range(2) for k in range(NZL)]
    for i in range(1, len(steps) + 2):
        if i < len(steps):
            stage_a(*steps[i])
        if i - 1 < len(steps):
            stage_b(*steps[i - 1])
        if i >= 2:
            stage_c(*steps[i - 2])

    keys = acck[...].astype(BF16)
    values = accv[...].astype(BF16)
    size = ROWS // CHUNKS
    for i in range(CHUNKS):
        part = pl.ds(i * size, size)
        scores = lax.dot_general(q[part], keys, (((1,), (1,)), ((), ())),
                                 preferred_element_type=F32) * HEAD_DIM ** (-0.5)
        top = jnp.max(scores, axis=1, keepdims=True)
        raised = jnp.exp(scores - top)
        probs = (raised / jnp.sum(raised, axis=1, keepdims=True)).astype(BF16)
        ctx[part] = jnp.dot(probs, values, preferred_element_type=F32).astype(BF16)
        remote(ctx.at[part], out_hbm.at[0, part], o_send, o_recv, nxt, mp).start()

    for h in range(2):
        whole = p[h].at[pl.ds(0, PLANE - 1)]
        pltpu.make_async_copy(whole, whole, s1_send.at[h]).wait()
        pltpu.make_async_copy(whole, whole, s3_send.at[h]).wait()
        two = cc[h].at[pl.ds(0, 2)]
        pltpu.make_async_copy(two, two, s2_send.at[h]).wait()
        pltpu.make_async_copy(e.at[h, pl.ds(0, 3)], e.at[h, pl.ds(0, 3)], z_send.at[h]).wait()
        pltpu.make_async_copy(e.at[h, pl.ds(0, 12)], e.at[h, pl.ds(0, 12)], x_send.at[h]).wait()
    pltpu.make_async_copy(ctx, ctx, o_send).wait()
    pltpu.make_async_copy(ctx, out_hbm.at[0], o_recv).wait()


def per_device(queries, encoded, key_weight, value_weight, owner):
    wk = key_weight.reshape(NZL * NX, 2, HALF, HEAD_DIM)
    wv = value_weight.reshape(NZL * NX, 2, HALF, HEAD_DIM)
    dma = pltpu.SemaphoreType.DMA
    return pl.pallas_call(
        kernel,
        out_shape=jax.ShapeDtypeStruct((1, ROWS, HEAD_DIM), BF16),
        in_specs=[pl.BlockSpec(memory_space=pl.ANY)] * 5,
        out_specs=pl.BlockSpec(memory_space=pl.ANY),
        scratch_shapes=[
            pltpu.SMEM((MICRO,), jnp.int32),
            pltpu.VMEM((ROWS, HEAD_DIM), BF16),
            pltpu.VMEM((2, NZL * NX, HALF, HEAD_DIM), BF16),
            pltpu.VMEM((2, NZL * NX, HALF, HEAD_DIM), BF16),
            pltpu.VMEM((PLANE, PIECE, HALF), BF16),
            pltpu.VMEM((PLANE, PIECE, HALF), BF16),
            pltpu.VMEM((NZH, MICRO, PIECE, HALF), BF16),
            pltpu.VMEM((NZH, MICRO, PIECE, HALF), BF16),
            pltpu.VMEM((2, MICRO, PIECE, HALF), BF16),
            pltpu.VMEM((2, NZL * NX, ROWS, HALF), BF16),
            pltpu.VMEM((ROWS, HEAD_DIM), F32),
            pltpu.VMEM((ROWS, HEAD_DIM), F32),
            pltpu.VMEM((ROWS, HEAD_DIM), BF16),
            dma, dma, dma((2, 2)),
            dma((2,)), dma((2,)), dma((2,)), dma((2,)), dma((2,)), dma((2,)),
            dma((2,)), dma((2,)), dma((2, NZL * NX)), dma, dma,
        ],
        compiler_params=pltpu.CompilerParams(
            collective_id=0, has_side_effects=True, vmem_limit_bytes=32 * 1024 * 1024),
        cost_estimate=pl.CostEstimate(
            flops=2 * 2 * 256 * 4096 * 256, bytes_accessed=5 * 1024 * 1024, transcendentals=65536),
    )(queries, encoded, wk, wv, owner)


def solution(mesh):
    placed = (
        P("section", None, "mp"),
        P("section", None, "mp"),
        P("section", None, "mp"),
        P("section", None, "mp"),
        P(),
    )
    return jax.shard_map(
        per_device, mesh=mesh, in_specs=placed, out_specs=P("section", None, "mp"), check_vma=False
    )
```

time: 262 us -> 74.7 us (0.29)
  the two profiles are of different devices: /device:TPU:102 before, /device:TPU:4 now
where the time goes in v1:
time: 74.7 us; the launch traced here: 74.4 us
  Pallas kernels  68.1 us (91%)
  local copies, waits for them, and re-layouts  6.3 us (8%)
    pallas_call x1, Pallas kernels, per_device(): pl.pallas_call(kernel, out_shape=jax.ShapeDtypeStruct((1, ROWS, HEAD_DIM)...  68.1 us
    unnamed x11, local copies, waits for them, and re-layouts  6.3 us

profile of v1, /device:TPU:4, one launch (start us, length us, event | category | flops | bytes accessed | tf_op | source)
XLA Modules:
  0.0 74.4 jit_solution(17368735135766412934)
XLA Ops:
  0.0 0.0 copy-start
  0.0 1.6 %copy-done = bf16[1,4096,256]{2,1,0:T(8,128)(2,1)S(1)} copy-done((bf16[1,4096,256]{2,1,0:T(8,128)(2,1)S(1)}, bf16[1,4096,256]{2,1,0:T(8,128)(2,1)}, u32[]{:S(2)}) %copy-start) | copy-done | bytes 2097176
  1.6 0.0 copy-start.1
  1.6 1.6 %copy-done.1 = bf16[1,4096,256]{2,1,0:T(8,128)(2,1)S(1)} copy-done((bf16[1,4096,256]{2,1,0:T(8,128)(2,1)S(1)}, bf16[1,4096,256]{2,1,0:T(8,128)(2,1)}, u32[]{:S(2)}) %copy-start.1) | copy-done | bytes 2097176
  3.2 0.0 copy-start.2
  3.2 0.9 %copy-done.2 = bf16[1,256,256]{2,1,0:T(8,128)(2,1)S(1)} copy-done((bf16[1,256,256]{2,1,0:T(8,128)(2,1)S(1)}, bf16[1,256,256]{2,1,0:T(8,128)(2,1)}, u32[]{:S(2)}) %copy-start.2) | copy-done | bytes 131096
  4.1 0.0 copy-start.3
  4.1 0.9 %copy-done.3 = bf16[1,256,256]{2,1,0:T(8,128)(2,1)S(1)} copy-done((bf16[1,256,256]{2,1,0:T(8,128)(2,1)S(1)}, bf16[1,256,256]{2,1,0:T(8,128)(2,1)}, u32[]{:S(2)}) %copy-start.3) | copy-done | bytes 131096
  5.0 0.0 copy-start.4
  5.0 0.7 copy-done.4
  5.6 68.1 %shard_map.55 = bf16[1,256,256]{2,1,0:T(8,128)(2,1)S(1)} custom-call(bf16[1,256,256]{2,1,0:T(8,128)(2,1)S(1)} %copy-done.2, bf16[1,256,256]{2,1,0:T(8,128)(2,1)S(1)} %copy-done.3, bf16[16,2,128,256]{3,2,1,0:T(8,128)(2,1)S(1)} %bitcast.2, bf16[16,2,128,256]{3,2,1,0:T(8,128)(2,1)S(1)} %bitcast.3, s32[8]{0:T(128)S(1)} %copy-done.4), custom_call_target="tpu_custom_call" | custom-call | flops 1073741824 | bytes 5242880 | tf_op jit(solution)/shard_map/pallas_call | solution.py:211
  73.8 0.7 copy.7
Async XLA Ops:
  0.0 1.6 %copy-start = (bf16[1,4096,256]{2,1,0:T(8,128)(2,1)S(1)}, bf16[1,4096,256]{2,1,0:T(8,128)(2,1)}, u32[]{:S(2)}) copy-start(bf16[1,4096,256]{2,1,0:T(8,128)(2,1)} %param.7) | copy-start | bytes 6291460
  1.6 1.6 %copy-start.1 = (bf16[1,4096,256]{2,1,0:T(8,128)(2,1)S(1)}, bf16[1,4096,256]{2,1,0:T(8,128)(2,1)}, u32[]{:S(2)}) copy-start(bf16[1,4096,256]{2,1,0:T(8,128)(2,1)} %param.8) | copy-start | bytes 6291460
  3.2 0.9 %copy-start.2 = (bf16[1,256,256]{2,1,0:T(8,128)(2,1)S(1)}, bf16[1,256,256]{2,1,0:T(8,128)(2,1)}, u32[]{:S(2)}) copy-start(bf16[1,256,256]{2,1,0:T(8,128)(2,1)} %q_hbm.1) | copy-start | bytes 393220
  4.1 0.9 %copy-start.3 = (bf16[1,256,256]{2,1,0:T(8,128)(2,1)S(1)}, bf16[1,256,256]{2,1,0:T(8,128)(2,1)}, u32[]{:S(2)}) copy-start(bf16[1,256,256]{2,1,0:T(8,128)(2,1)} %e_hbm.1) | copy-start | bytes 393220
  5.0 0.7 copy-start.4

commit v2 on v1

v2 whole, which is shorter than its diff:
```python
import jax
import jax.numpy as jnp
from jax import lax
from jax.experimental import pallas as pl
from jax.experimental.pallas import tpu as pltpu
from jax.sharding import PartitionSpec as P

MESH = pl.DeviceIdType.MESH
HEAD_DIM = 256
MICRO = 8
NY, NZH, NC = 8, 3, 2
NZL, NX = 4, 4
PLANE = NY * NC
ROWS = 256
PIECE = ROWS // PLANE
HALF = 128
CHUNKS = 4
ORDER = (
    "A0", "A1", "A2", "A3", "B0", "B1", "A4", "A5", "B2", "A6", "B3", "A7", "W",
    "C0", "B4", "C1", "B5", "C2", "B6", "C3", "B7", "C4", "C5", "C6", "C7",
)
F32 = jnp.float32
BF16 = jnp.bfloat16


def kernel(q_hbm, e_hbm, wk_hbm, wv_hbm, owner_hbm, out_hbm,
           owner, q, el, wk, wv, p0, p1, c0, c1, f, e, acck, accv, ctx,
           own_sem, el_sem, q_sem, w_sem, s1_send, s1_recv, s2_send, s2_recv, s3_send, s3_recv,
           z_send, x_send, g_recv, o_send, o_recv):
    sec = lax.axis_index("section")
    mp = lax.axis_index("mp")
    y, zh, c = lax.div(sec, 6), lax.rem(lax.div(sec, 2), 3), lax.rem(sec, 2)
    zl, x = lax.div(mp, 4), lax.rem(mp, 4)
    place = y * 2 + c
    right = zl * 4 + lax.rem(x + 1, 4)
    left = zl * 4 + lax.rem(x + 3, 4)
    nxt = lax.rem(sec + 1, 48)
    prv = lax.rem(sec + 47, 48)
    p, cc = (p0, p1), (c0, c1)

    mates = []
    for dy in (4, 3, 5, 2, 6, 1, 7, 0):
        yy = y + dy
        yy = yy - NY * lax.div(yy, NY)
        pair = lax.rem(zh + NY - yy, 4) * 2
        for cc_ in ((c, 1 - c) if dy else (1 - c,)):
            mates.append((yy * 2 + cc_, yy * 6 + zh * 2 + cc_, pair + cc_))

    def beside(k):
        return y * 6 + lax.rem(zh + k, 3) * 2 + c

    half_of_run = lax.div(zl, 2)
    inner = lax.rem(zl + half_of_run, 2)

    def mirrored(v):
        return v + half_of_run * (3 - 2 * v)

    def line(k):
        return zl if k == 0 else mirrored(1 - inner if k == 1 else k)

    def onward(k):
        return mirrored(2 if k == 1 else 0)

    def remote(src, dst, ssem, rsem, section, model):
        return pltpu.make_async_remote_copy(
            src_ref=src, dst_ref=dst, send_sem=ssem, recv_sem=rsem,
            device_id=(section, model), device_id_type=MESH)

    barrier = pltpu.get_barrier_semaphore()

    def greet(section, model):
        pl.semaphore_signal(barrier, inc=1, device_id=(section, model), device_id_type=MESH)

    greet(beside(1), mp)
    greet(beside(2), mp)
    for _, section, _ in mates:
        greet(section, mp)
    greet(prv, mp)
    greet(sec, lax.rem(zl + 1, 4) * 4 + x)
    greet(sec, lax.rem(zl + 3, 4) * 4 + x)
    greet(sec, right)
    greet(sec, left)

    el_copy = pltpu.make_async_copy(e_hbm.at[0], el, el_sem)
    el_copy.start()
    own_copy = pltpu.make_async_copy(owner_hbm, owner, own_sem)
    own_copy.start()
    loads = [pltpu.make_async_copy(q_hbm.at[0], q, q_sem)]
    for h in range(2):
        loads.append(pltpu.make_async_copy(wk_hbm.at[:, h], wk.at[h], w_sem.at[0, h]))
        loads.append(pltpu.make_async_copy(wv_hbm.at[:, h], wv.at[h], w_sem.at[1, h]))
    for load in loads:
        load.start()
    el_copy.wait()
    mine = pl.ds(pl.multiple_of(place * PIECE, PIECE), PIECE)
    for h in range(2):
        p[h][place] = el[mine, h * HALF:(h + 1) * HALF]
    acck[...] = jnp.zeros_like(acck)
    accv[...] = jnp.zeros_like(accv)
    own_copy.wait()
    at_place, at_zh = [], []
    for m in range(MICRO):
        o = owner[m]
        at_place.append(lax.div(o, 6) * 2 + lax.rem(o, 2))
        at_zh.append(lax.rem(lax.div(o, 2), 3))
    pl.semaphore_wait(barrier, PLANE - 1 + 2 + 2 + 2 + 1)

    for h in range(2):
        for t, section, _ in mates:
            remote(el.at[pl.ds(pl.multiple_of(t * PIECE, PIECE), PIECE), pl.ds(h * HALF, HALF)],
                   p[h].at[place], s1_send.at[h], s1_recv.at[h], section, mp).start()

    for h in range(2):
        whole = p[h].at[pl.ds(0, PLANE - 1)]
        pltpu.make_async_copy(whole, whole, s1_recv.at[h]).wait()
        for m in range(MICRO):
            cc[h][zh, m] = p[h][at_place[m]]
        for k in (1, 2):
            remote(cc[h].at[zh], cc[h].at[zh], s2_send.at[h], s2_recv.at[h], beside(k), mp).start()

    for h in range(2):
        pltpu.make_async_copy(cc[h].at[pl.ds(0, 2)], cc[h].at[pl.ds(0, 2)], s2_recv.at[h]).wait()
        for m in range(MICRO):
            f[h, m] = cc[h][at_zh[m], m]
        for _, section, m in mates:
            remote(f.at[h, m], e.at[h, mp, mine], s3_send.at[h], s3_recv.at[h], section, mp).start()
        e[h, mp, mine] = f[h, lax.rem(sec, MICRO)]

    def block(h, j):
        return e.at[h, j]

    def arrived(h, j):
        pltpu.make_async_copy(block(h, j), block(h, j), g_recv.at[h, j]).wait()

    def to_x(h, j, model):
        remote(block(h, j), block(h, j), x_send.at[h], g_recv.at[h, j], sec, model).start()

    def to_z(h, j, run):
        remote(block(h, j), block(h, j), z_send.at[h], g_recv.at[h, j], sec, run * 4 + x).start()

    def stage_a(h, k):
        j = line(k) * 4 + x
        if k == 0:
            others = e.at[h, mp, pl.ds(0, ROWS - PIECE)]
            pltpu.make_async_copy(others, others, s3_recv.at[h]).wait()

            @pl.when(zl < NZL - 1)
            def _():
                to_z(h, j, zl + 1)

            @pl.when(zl > 0)
            def _():
                to_z(h, j, zl - 1)
        else:
            arrived(h, j)

            @pl.when(inner == 1)
            def _():
                to_z(h, j, onward(k))

        to_x(h, j, right)
        to_x(h, j, left)

    def stage_b(h, k):
        j = line(k) * 4
        from_left = j + lax.rem(x + 3, 4)
        from_right = j + lax.rem(x + 1, 4)
        if k % 2 == 0:
            arrived(h, from_left)
            to_x(h, from_left, right)
            arrived(h, from_right)
        else:
            arrived(h, from_right)
            to_x(h, from_right, left)
            arrived(h, from_left)

    def stage_c(h, k):
        j = line(k) * 4
        arrived(h, j + lax.rem(x + 2, 4))
        left_side = jnp.concatenate([e[h, j + i] for i in range(NX)], axis=1)
        for w, acc in ((wk, acck), (wv, accv)):
            rows = w[h, pl.ds(j, NX)].reshape(NX * HALF, HEAD_DIM)
            acc[...] += jnp.dot(left_side, rows, preferred_element_type=F32)

    steps = [(h, k) for k in range(NZL) for h in range(2)]
    for step in ORDER:
        if step == "W":
            for load in loads:
                load.wait()
        else:
            {"A": stage_a, "B": stage_b, "C": stage_c}[step[0]](*steps[int(step[1])])

    keys = acck[...].astype(BF16)
    values = accv[...].astype(BF16)
    size = ROWS // CHUNKS
    for i in range(CHUNKS):
        part = pl.ds(i * size, size)
        scores = lax.dot_general(q[part], keys, (((1,), (1,)), ((), ())),
                                 preferred_element_type=F32) * HEAD_DIM ** (-0.5)
        top = jnp.max(scores, axis=1, keepdims=True)
        raised = jnp.exp(scores - top)
        probs = (raised / jnp.sum(raised, axis=1, keepdims=True)).astype(BF16)
        ctx[part] = jnp.dot(probs, values, preferred_element_type=F32).astype(BF16)
        remote(ctx.at[part], out_hbm.at[0, part], o_send, o_recv, nxt, mp).start()

    for h in range(2):
        whole = p[h].at[pl.ds(0, PLANE - 1)]
        pltpu.make_async_copy(whole, whole, s1_send.at[h]).wait()
        pltpu.make_async_copy(whole, whole, s3_send.at[h]).wait()
        two = cc[h].at[pl.ds(0, 2)]
        pltpu.make_async_copy(two, two, s2_send.at[h]).wait()
        one = e.at[h, 0]
        pltpu.make_async_copy(one, one, z_send.at[h]).wait()

        @pl.when(inner == 1)
        def _():
            four = e.at[h, pl.ds(0, 4)]
            pltpu.make_async_copy(four, four, z_send.at[h]).wait()

        pltpu.make_async_copy(e.at[h, pl.ds(0, 12)], e.at[h, pl.ds(0, 12)], x_send.at[h]).wait()
    pltpu.make_async_copy(ctx, ctx, o_send).wait()
    pltpu.make_async_copy(ctx, out_hbm.at[0], o_recv).wait()


def per_device(queries, encoded, key_weight, value_weight, owner):
    wk = key_weight.reshape(NZL * NX, 2, HALF, HEAD_DIM)
    wv = value_weight.reshape(NZL * NX, 2, HALF, HEAD_DIM)
    dma = pltpu.SemaphoreType.DMA
    return pl.pallas_call(
        kernel,
        out_shape=jax.ShapeDtypeStruct((1, ROWS, HEAD_DIM), BF16),
        in_specs=[pl.BlockSpec(memory_space=pl.ANY)] * 5,
        out_specs=pl.BlockSpec(memory_space=pl.ANY),
        scratch_shapes=[
            pltpu.SMEM((MICRO,), jnp.int32),
            pltpu.VMEM((ROWS, HEAD_DIM), BF16),
            pltpu.VMEM((ROWS, HEAD_DIM), BF16),
            pltpu.VMEM((2, NZL * NX, HALF, HEAD_DIM), BF16),
            pltpu.VMEM((2, NZL * NX, HALF, HEAD_DIM), BF16),
            pltpu.VMEM((PLANE, PIECE, HALF), BF16),
            pltpu.VMEM((PLANE, PIECE, HALF), BF16),
            pltpu.VMEM((NZH, MICRO, PIECE, HALF), BF16),
            pltpu.VMEM((NZH, MICRO, PIECE, HALF), BF16),
            pltpu.VMEM((2, MICRO, PIECE, HALF), BF16),
            pltpu.VMEM((2, NZL * NX, ROWS, HALF), BF16),
            pltpu.VMEM((ROWS, HEAD_DIM), F32),
            pltpu.VMEM((ROWS, HEAD_DIM), F32),
            pltpu.VMEM((ROWS, HEAD_DIM), BF16),
            dma, dma, dma, dma((2, 2)),
            dma((2,)), dma((2,)), dma((2,)), dma((2,)), dma((2,)), dma((2,)),
            dma((2,)), dma((2,)), dma((2, NZL * NX)), dma, dma,
        ],
        compiler_params=pltpu.CompilerParams(
            collective_id=0, has_side_effects=True, vmem_limit_bytes=60 * 1024 * 1024),
        cost_estimate=pl.CostEstimate(
            flops=2 * 2 * 256 * 4096 * 256, bytes_accessed=5 * 1024 * 1024, transcendentals=65536),
    )(queries, encoded, wk, wv, owner)


def solution(mesh):
    placed = (
        P("section", None, "mp"),
        P("section", None, "mp"),
        P("section", None, "mp"),
        P("section", None, "mp"),
        P(),
    )
    return jax.shard_map(
        per_device, mesh=mesh, in_specs=placed, out_specs=P("section", None, "mp"), check_vma=False
    )
```

time: 74.7 us -> 66.3 us (0.89)
  the two profiles are of different devices: /device:TPU:4 before, /device:TPU:128 now
where the time goes in v2:
time: 66.3 us; the launch traced here: 66.1 us
  Pallas kernels  64.5 us (97%)
  local copies, waits for them, and re-layouts  1.57 us (2%)
    pallas_call x1, Pallas kernels, per_device(): pl.pallas_call(kernel, out_shape=jax.ShapeDtypeStruct((1, ROWS, HEAD_DIM)...  64.5 us
    unnamed x1, local copies, waits for them, and re-layouts  1.57 us

profile of v2, /device:TPU:128, one launch (start us, length us, event | category | flops | bytes accessed | tf_op | source)
XLA Modules:
  0.0 66.1 jit_solution(8417560267039522506)
XLA Ops:
  0.0 64.5 %shard_map.55 = bf16[1,256,256]{2,1,0:T(8,128)(2,1)} custom-call(bf16[1,256,256]{2,1,0:T(8,128)(2,1)} %q_hbm.1, bf16[1,256,256]{2,1,0:T(8,128)(2,1)} %e_hbm.1, bf16[16,2,128,256]{3,2,1,0:T(8,128)(2,1)} %bitcast.2, bf16[16,2,128,256]{3,2,1,0:T(8,128)(2,1)} %bitcast.3, s32[8]{0:T(128)} %owner_hbm.1), custom_call_target="tpu_custom_call" | custom-call | flops 1073741824 | bytes 5242880 | tf_op jit(solution)/shard_map/pallas_call | solution.py:229
  64.5 1.6 %copy.7 = bf16[1,256,256]{2,1,0:T(8,128)(2,1)} copy(bf16[1,256,256]{2,1,0:T(8,128)(2,1)} %shard_map.55) | data formatting | bytes 262144

commit v3 on v2

--- a/solution.py
+++ b/solution.py
@@ -14,10 +14,11 @@
 ROWS = 256
 PIECE = ROWS // PLANE
 HALF = 128
-CHUNKS = 4
+CHUNKS = 2
 ORDER = (
-    "A0", "A1", "A2", "A3", "B0", "B1", "A4", "A5", "B2", "A6", "B3", "A7", "W",
-    "C0", "B4", "C1", "B5", "C2", "B6", "C3", "B7", "C4", "C5", "C6", "C7",
+    "P0", "P1", "N", "Q0", "Q1", "R0", "R1", "A0", "A1", "A2", "A3", "B0", "B1",
+    "A4", "A5", "B2", "A6", "B3", "A7", "W", "C0", "B4", "C1", "B5", "C2", "B6",
+    "C3", "B7", "C4", "C5", "C6", "C7",
 )
 F32 = jnp.float32
 BF16 = jnp.bfloat16
@@ -71,46 +72,48 @@
     def greet(section, model):
         pl.semaphore_signal(barrier, inc=1, device_id=(section, model), device_id_type=MESH)
 
+    el_copy = pltpu.make_async_copy(e_hbm.at[0], el, el_sem)
+    el_copy.start()
+    own_copy = pltpu.make_async_copy(owner_hbm, owner, own_sem)
+    own_copy.start()
+    for _, section, _ in mates:
+        greet(section, mp)
     greet(beside(1), mp)
     greet(beside(2), mp)
-    for _, section, _ in mates:
-        greet(section, mp)
     greet(prv, mp)
     greet(sec, lax.rem(zl + 1, 4) * 4 + x)
     greet(sec, lax.rem(zl + 3, 4) * 4 + x)
     greet(sec, right)
     greet(sec, left)
-
-    el_copy = pltpu.make_async_copy(e_hbm.at[0], el, el_sem)
-    el_copy.start()
-    own_copy = pltpu.make_async_copy(owner_hbm, owner, own_sem)
-    own_copy.start()
     loads = [pltpu.make_async_copy(q_hbm.at[0], q, q_sem)]
     for h in range(2):
         loads.append(pltpu.make_async_copy(wk_hbm.at[:, h], wk.at[h], w_sem.at[0, h]))
         loads.append(pltpu.make_async_copy(wv_hbm.at[:, h], wv.at[h], w_sem.at[1, h]))
-    for load in loads:
-        load.start()
+    mine = pl.ds(pl.multiple_of(place * PIECE, PIECE), PIECE)
+    at_place, at_zh = [], []
+
+    def stage_n():
+        for load in loads:
+            load.start()
+        for h in range(2):
+            p[h][place] = el[mine, h * HALF:(h + 1) * HALF]
+        acck[...] = jnp.zeros_like(acck)
+        accv[...] = jnp.zeros_like(accv)
+        own_copy.wait()
+        for m in range(MICRO):
+            o = owner[m]
+            at_place.append(lax.div(o, 6) * 2 + lax.rem(o, 2))
+            at_zh.append(lax.rem(lax.div(o, 2), 3))
+
     el_copy.wait()
-    mine = pl.ds(pl.multiple_of(place * PIECE, PIECE), PIECE)
-    for h in range(2):
-        p[h][place] = el[mine, h * HALF:(h + 1) * HALF]
-    acck[...] = jnp.zeros_like(acck)
-    accv[...] = jnp.zeros_like(accv)
-    own_copy.wait()
-    at_place, at_zh = [], []
-    for m in range(MICRO):
-        o = owner[m]
-        at_place.append(lax.div(o, 6) * 2 + lax.rem(o, 2))
-        at_zh.append(lax.rem(lax.div(o, 2), 3))
     pl.semaphore_wait(barrier, PLANE - 1 + 2 + 2 + 2 + 1)
 
-    for h in range(2):
+    def stage_p(h):
         for t, section, _ in mates:
             remote(el.at[pl.ds(pl.multiple_of(t * PIECE, PIECE), PIECE), pl.ds(h * HALF, HALF)],
                    p[h].at[place], s1_send.at[h], s1_recv.at[h], section, mp).start()
 
-    for h in range(2):
+    def stage_q(h):
         whole = p[h].at[pl.ds(0, PLANE - 1)]
         pltpu.make_async_copy(whole, whole, s1_recv.at[h]).wait()
         for m in range(MICRO):
@@ -118,8 +121,9 @@
         for k in (1, 2):
             remote(cc[h].at[zh], cc[h].at[zh], s2_send.at[h], s2_recv.at[h], beside(k), mp).start()
 
-    for h in range(2):
-        pltpu.make_async_copy(cc[h].at[pl.ds(0, 2)], cc[h].at[pl.ds(0, 2)], s2_recv.at[h]).wait()
+    def stage_r(h):
+        two = cc[h].at[pl.ds(0, 2)]
+        pltpu.make_async_copy(two, two, s2_recv.at[h]).wait()
         for m in range(MICRO):
             f[h, m] = cc[h][at_zh[m], m]
         for _, section, m in mates:
@@ -163,19 +167,18 @@
 
     def stage_b(h, k):
         j = line(k) * 4
-        from_left = j + lax.rem(x + 3, 4)
-        from_right = j + lax.rem(x + 1, 4)
-        if k % 2 == 0:
-            arrived(h, from_left)
-            to_x(h, from_left, right)
-            arrived(h, from_right)
+        if (h + k) % 2 == 0:
+            j += lax.rem(x + 3, 4)
+            arrived(h, j)
+            to_x(h, j, right)
         else:
-            arrived(h, from_right)
-            to_x(h, from_right, left)
-            arrived(h, from_left)
+            j += lax.rem(x + 1, 4)
+            arrived(h, j)
+            to_x(h, j, left)
 
     def stage_c(h, k):
         j = line(k) * 4
+        arrived(h, j + lax.rem(x + (1 if (h + k) % 2 == 0 else 3), 4))
         arrived(h, j + lax.rem(x + 2, 4))
         left_side = jnp.concatenate([e[h, j + i] for i in range(NX)], axis=1)
         for w, acc in ((wk, acck), (wv, accv)):
@@ -187,6 +190,10 @@
         if step == "W":
             for load in loads:
                 load.wait()
+        elif step == "N":
+            stage_n()
+        elif step[0] in "PQR":
+            {"P": stage_p, "Q": stage_q, "R": stage_r}[step[0]](int(step[1]))
         else:
             {"A": stage_a, "B": stage_b, "C": stage_c}[step[0]](*steps[int(step[1])])
 

time: 66.3 us -> 65.3 us (0.985)
  the two profiles are of different devices: /device:TPU:128 before, /device:TPU:4 now
where the time goes in v3:
time: 65.3 us; the launch traced here: 65.1 us
  Pallas kernels  63.5 us (97%)
  local copies, waits for them, and re-layouts  1.57 us (2%)
    pallas_call x1, Pallas kernels, per_device(): pl.pallas_call(kernel, out_shape=jax.ShapeDtypeStruct((1, ROWS, HEAD_DIM)...  63.5 us
    unnamed x1, local copies, waits for them, and re-layouts  1.57 us

profile of v3, /device:TPU:4, one launch (start us, length us, event | category | flops | bytes accessed | tf_op | source)
XLA Modules:
  0.0 65.1 jit_solution(8273811303205868710)
XLA Ops:
  0.0 63.5 %shard_map.55 = bf16[1,256,256]{2,1,0:T(8,128)(2,1)} custom-call(bf16[1,256,256]{2,1,0:T(8,128)(2,1)} %q_hbm.1, bf16[1,256,256]{2,1,0:T(8,128)(2,1)} %e_hbm.1, bf16[16,2,128,256]{3,2,1,0:T(8,128)(2,1)} %bitcast.2, bf16[16,2,128,256]{3,2,1,0:T(8,128)(2,1)} %bitcast.3, s32[8]{0:T(128)} %owner_hbm.1), custom_call_target="tpu_custom_call" | custom-call | flops 1073741824 | bytes 5242880 | tf_op jit(solution)/shard_map/pallas_call | solution.py:236
  63.5 1.6 %copy.7 = bf16[1,256,256]{2,1,0:T(8,128)(2,1)} copy(bf16[1,256,256]{2,1,0:T(8,128)(2,1)} %shard_map.55) | data formatting | bytes 262144

commit v4 on v3

--- a/solution.py
+++ b/solution.py
@@ -16,9 +16,9 @@
 HALF = 128
 CHUNKS = 2
 ORDER = (
-    "P0", "P1", "N", "Q0", "Q1", "R0", "R1", "A0", "A1", "A2", "A3", "B0", "B1",
-    "A4", "A5", "B2", "A6", "B3", "A7", "W", "C0", "B4", "C1", "B5", "C2", "B6",
-    "C3", "B7", "C4", "C5", "C6", "C7",
+    "P0", "P1", "N", "Q0", "Q1", "R0", "R1", "A0", "A1", "A2", "B0", "A3", "B1",
+    "A4", "A5", "B2", "A6", "B3", "A7", "B4", "W", "C0", "B5", "C1", "B6", "C2",
+    "B7", "C3", "C4", "C5", "C6", "C7",
 )
 F32 = jnp.float32
 BF16 = jnp.bfloat16

time: 65.3 us -> 65 us (level)
  the two profiles are of different devices: /device:TPU:4 before, /device:TPU:192 now
where the time goes in v4:
time: 65 us; the launch traced here: 64.9 us
  Pallas kernels  63.3 us (97%)
  local copies, waits for them, and re-layouts  1.57 us (2%)
    pallas_call x1, Pallas kernels, per_device(): pl.pallas_call(kernel, out_shape=jax.ShapeDtypeStruct((1, ROWS, HEAD_DIM)...  63.3 us
    unnamed x1, local copies, waits for them, and re-layouts  1.57 us

profile of v4, /device:TPU:192, one launch (start us, length us, event | category | flops | bytes accessed | tf_op | source)
XLA Modules:
  0.0 64.9 jit_solution(705604679714710046)
XLA Ops:
  0.0 63.3 %shard_map.55 = bf16[1,256,256]{2,1,0:T(8,128)(2,1)} custom-call(bf16[1,256,256]{2,1,0:T(8,128)(2,1)} %q_hbm.1, bf16[1,256,256]{2,1,0:T(8,128)(2,1)} %e_hbm.1, bf16[16,2,128,256]{3,2,1,0:T(8,128)(2,1)} %bitcast.2, bf16[16,2,128,256]{3,2,1,0:T(8,128)(2,1)} %bitcast.3, s32[8]{0:T(128)} %owner_hbm.1), custom_call_target="tpu_custom_call" | custom-call | flops 1073741824 | bytes 5242880 | tf_op jit(solution)/shard_map/pallas_call | solution.py:236
  63.3 1.6 %copy.7 = bf16[1,256,256]{2,1,0:T(8,128)(2,1)} copy(bf16[1,256,256]{2,1,0:T(8,128)(2,1)} %shard_map.55) | data formatting | bytes 262144
